TPU v7x, 32 devices: a whole 2x2x4 slice. The times are simulated.
32 devices in a mesh: groups: 1, res: 16 (over z, y, core), chan: 2 (over x).
Axes of the slice: x: 2, y: 2, z: 4, core: 2. Of those that a mesh axis runs over, the one named last changes fastest.
Arguments:
- pair: bfloat16 [128, 256, 256], P(('groups', 'chan'), 'res'), may hold values from -6 to 6
- pair_mask: int32 [256, 256], P(('groups', 'res'), 'chan'), may hold values from 0 to 1, as said below
- norm_gain: float32 [128], replicated, may hold values from 0.1 to 1.9
- norm_bias: float32 [128], replicated, may hold values from -3 to 3
- w_edges: bfloat16 [128, 512], replicated, may hold values from -0.5 to 0.5
- w_gate: bfloat16 [128, 128], replicated, may hold values from -0.5 to 0.5
- out_gain: float32 [128], replicated, may hold values from 0.1 to 1.9
- out_bias: float32 [128], replicated, may hold values from -3 to 3
- w_out: bfloat16 [128, 128], replicated, may hold values from -0.5 to 0.5
Outputs:
- update: bfloat16 [128, 256, 256], P('groups', 'res', 'chan')
Inputs may be any that keep to these rules, and one draw needn't show every extreme that they name: pair_mask[i, k] = v[i] v[k] for a token vector v that is 1 on a prefix of at least 128 tokens and 0 on the rest, with at least one token invalid.
All inputs are finite; a program needn't handle non-finite values.
Results may differ from a plain program's by a relative error of at most 0.0058.
Values may be sent and summed in bfloat16 or wider, within the bound.
A program may use at most 64 MiB of HBM per device.

v0:
```python
import jax
import jax.numpy as jnp
from jax import lax
from jax.sharding import PartitionSpec as P

epsilon = 1e-05


def layer_norm(values, scale_gain, shift_bias):
    average = jnp.mean(values, axis=0, keepdims=True)
    centered = values - average
    variance = jnp.mean(centered * centered, axis=0, keepdims=True)
    return (
        centered * lax.rsqrt(variance + epsilon) * scale_gain[:, None, None]
        + shift_bias[:, None, None]
    )


def project_edges(normed, mask_block, w_edges):
    hidden = w_edges.shape[1] // 4
    maskf = mask_block.astype(jnp.float32)[None]

    def edge_half(offset):
        gate_part = jnp.einsum(
            "cij,ch->hij",
            normed,
            w_edges[:, offset : offset + hidden],
            preferred_element_type=jnp.float32,
        )
        value_part = jnp.einsum(
            "cij,ch->hij",
            normed,
            w_edges[:, offset + hidden : offset + 2 * hidden],
            preferred_element_type=jnp.float32,
        )
        return (jax.nn.sigmoid(gate_part) * value_part * maskf).astype(jnp.bfloat16)

    return (edge_half(0), edge_half(2 * hidden))


def body(pair, pair_mask, norm_gain, norm_bias, w_edges, w_gate, out_gain, out_bias, w_out):
    quarter = pair_mask.shape[1]
    whole_rows, mask_rows = (
        lax.all_gather(pair, "chan", axis=0, tiled=True),
        lax.all_gather(pair_mask, "chan", axis=1, tiled=True),
    )
    normed_rows = layer_norm(whole_rows.astype(jnp.float32), norm_gain, norm_bias).astype(
        jnp.bfloat16
    )
    left_edges, right_edges = project_edges(normed_rows, mask_rows, w_edges)
    left_edges, right_edges = (
        lax.all_to_all(left_edges, "res", split_axis=0, concat_axis=1, tiled=True),
        lax.all_to_all(right_edges, "res", split_axis=0, concat_axis=1, tiled=True),
    )
    right_slice = lax.dynamic_slice_in_dim(
        right_edges, lax.axis_index("chan") * quarter, quarter, 1
    )
    product = jnp.einsum(
        "cik,cjk->cij", left_edges, right_slice, preferred_element_type=jnp.float32
    )
    normed = lax.dynamic_slice_in_dim(normed_rows, lax.axis_index("chan") * quarter, quarter, 2)
    returned = lax.all_to_all(
        product.astype(jnp.bfloat16), "res", split_axis=1, concat_axis=0, tiled=True
    )
    gate_values = jax.nn.sigmoid(
        jnp.einsum("cij,cd->dij", normed, w_gate, preferred_element_type=jnp.float32)
    )
    product_normed = layer_norm(returned.astype(jnp.float32), out_gain, out_bias).astype(
        jnp.bfloat16
    )
    mixed_out = jnp.einsum("hij,hd->dij", product_normed, w_out, preferred_element_type=jnp.float32)
    return (gate_values * mixed_out).astype(jnp.bfloat16)


def solution(mesh):
    return jax.shard_map(
        body,
        mesh=mesh,
        in_specs=(
            P(("groups", "chan"), "res", None),
            P(("groups", "res"), "chan"),
            P(),
            P(),
            P(),
            P(),
            P(),
            P(),
            P(),
        ),
        out_specs=P("groups", "res", "chan"),
        check_vma=False,
    )
```

profile of v0, /device:TPU:0, one launch (start us, length us, event | category | flops | bytes accessed | tf_op | source)
XLA Modules:
  0.0 132.5 jit_solution(1180828500531983529)
XLA Ops:
  6.5 0.7 all-gather.2.cloned.1.call-update
  7.3 5.5 %all_gather.7 = s32[16,256]{1,0:T(8,128)S(1)} all-gather(s32[16,128]{1,0:T(8,128)} %param.10), channel_id=1, replica_groups=mesh['groups'=1,'res'=16,'chan'=2] {'chan'}, dimensions={1}, use_global_device_ids=true | all-gather | bytes 24576 | tf_op jit(solution)/shard_map/all_gather | solution.py:45
  12.8 20.1 %all-gather.2.cloned.1.call-done = bf16[128,16,256]{2,1,0:T(8,128)(2,1)} async-done(((bf16[64,16,256]{2,1,0:T(8,128)(2,1)}), bf16[128,16,256]{2,1,0:T(8,128)(2,1)}) %all-gather.2.cloned.1.call-update) | async-done | bytes 1048592 | tf_op jit(solution)/shard_map/all_gather | solution.py:44
  32.9 1.9 %copy.31 = bf16[128,16,256]{0,2,1:T(8,128)(2,1)S(1)} copy(bf16[128,16,256]{2,1,0:T(8,128)(2,1)} %all-gather.2.cloned.1.call-done) | data formatting | bytes 2097152 | tf_op jit(solution)/shard_map/all_gather | solution.py:44
  34.9 0.3 convert_reduce_fusion
  35.3 1.3 fusion.2
  36.6 1.3 fusion.5
  37.9 0.4 fusion.25
  38.3 0.9 fusion.8
  39.2 1.7 %copy.34 = bf16[128,16,256]{2,1,0:T(8,128)(2,1)} copy(bf16[128,16,256]{0,2,1:T(8,128)(2,1)S(1)} %fusion.8) | data formatting | bytes 2097152 | tf_op jit(solution)/shard_map/convert_element_type | solution.py:36
  40.9 5.6 %all-to-all-start.1 = ((bf16[128,16,256]{2,1,0:T(8,128)(2,1)}), bf16[128,16,256]{2,1,0:T(8,128)(2,1)S(1)}, u32[]{:S(2)}, u32[]{:S(2)}) async-start(bf16[128,16,256]{2,1,0:T(8,128)(2,1)} %copy.34), calls=%async_computation.1 | async-start | bytes 2097152 | tf_op jit(solution)/shard_map/all_to_all | solution.py:53
  46.5 0.4 fusion.28
  46.9 0.9 fusion.7
  47.8 1.7 %copy.32 = bf16[128,16,256]{2,1,0:T(8,128)(2,1)} copy(bf16[128,16,256]{0,2,1:T(8,128)(2,1)S(1)} %fusion.7) | data formatting | bytes 2097152 | tf_op jit(solution)/shard_map/convert_element_type | solution.py:36
  49.6 19.9 %all-to-all-done.1 = bf16[128,16,256]{2,1,0:T(8,128)(2,1)S(1)} async-done(((bf16[128,16,256]{2,1,0:T(8,128)(2,1)}), bf16[128,16,256]{2,1,0:T(8,128)(2,1)S(1)}, u32[]{:S(2)}, u32[]{:S(2)}) %all-to-all-start.1) | async-done | bytes 1048608 | tf_op jit(solution)/shard_map/all_to_all | solution.py:53
  69.5 6.9 %all-to-all-start = ((bf16[128,16,256]{2,1,0:T(8,128)(2,1)}), bf16[128,16,256]{2,1,0:T(8,128)(2,1)S(1)}, u32[]{:S(2)}, u32[]{:S(2)}) async-start(bf16[128,16,256]{2,1,0:T(8,128)(2,1)} %copy.32), calls=%async_computation | async-start | bytes 2097152 | tf_op jit(solution)/shard_map/all_to_all | solution.py:52
  76.3 1.1 copy.35
  77.5 21.8 %all-to-all-done = bf16[128,16,256]{2,1,0:T(8,128)(2,1)S(1)} async-done(((bf16[128,16,256]{2,1,0:T(8,128)(2,1)}), bf16[128,16,256]{2,1,0:T(8,128)(2,1)S(1)}, u32[]{:S(2)}, u32[]{:S(2)}) %all-to-all-start) | async-done | bytes 1048608 | tf_op jit(solution)/shard_map/all_to_all | solution.py:52
  99.3 0.1 copy.33
  99.4 1.1 copy-done.1
  100.5 0.4 convolution_convert_fusion
  101.0 0.3 copy.36
  101.3 21.1 %all_to_all.45 = bf16[8,256,128]{2,0,1:T(8,128)(2,1)S(1)} all-to-all(bf16[8,256,128]{2,0,1:T(8,128)(2,1)S(1)} %copy.36), channel_id=1, replica_groups=mesh['groups'=1,'res'=16,'chan'=2] {'res'}, dimensions={1} | all-to-all | bytes 1048576 | tf_op jit(solution)/shard_map/all_to_all | solution.py:62
  122.4 0.2 fusion.37
  122.6 0.1 fusion.18
  122.8 0.2 multiply_reduce_fusion
  123.0 0.1 copy.38
  123.1 0.2 copy-done.3
  123.3 0.3 fusion.17
  123.6 0.3 fusion.19
  124.0 0.4 fusion.13
  124.5 1.2 copy.40
  (20 shorter events, 0.1 us)
Async XLA Ops:
  6.5 117.1 %copy-start = (bf16[128,128]{1,0:T(8,128)(2,1)S(1)}, bf16[128,128]{1,0:T(8,128)(2,1)}, u32[]{:S(2)}) copy-start(bf16[128,128]{1,0:T(8,128)(2,1)} %param.17) | copy-start | bytes 98308
  6.5 26.4 %all-gather.2.cloned.1.call-start = ((), (), s32[]{:S(2)}) async-start(), calls=%async_computation.3 | async-start | bytes 1572864 | tf_op jit(solution)/shard_map/all_gather | solution.py:44
  12.8 23.8 %copy-start.5 = (f32[128]{0:T(128)S(1)}, f32[128]{0:T(128)}, u32[]{:S(2)}) copy-start(f32[128]{0:T(128)} %param.12) | copy-start | bytes 1540
  12.8 23.8 %copy-start.6 = (f32[128]{0:T(128)S(1)}, f32[128]{0:T(128)}, u32[]{:S(2)}) copy-start(f32[128]{0:T(128)} %param.11) | copy-start | bytes 1540
  34.9 3.0 %copy-start.2 = (bf16[128,512]{1,0:T(8,128)(2,1)S(1)}, bf16[128,512]{1,0:T(8,128)(2,1)}, u32[]{:S(2)}) copy-start(bf16[128,512]{1,0:T(8,128)(2,1)} %param.13) | copy-start | bytes 393220
  40.9 28.6 %all-to-all-start.1 = ((bf16[128,16,256]{2,1,0:T(8,128)(2,1)}), bf16[128,16,256]{2,1,0:T(8,128)(2,1)S(1)}, u32[]{:S(2)}, u32[]{:S(2)}) async-start(bf16[128,16,256]{2,1,0:T(8,128)(2,1)} %copy.34), calls=%async_computation.1 | async-start | bytes 2097152 | tf_op jit(solution)/shard_map/all_to_all | solution.py:53
  69.5 29.8 %all-to-all-start = ((bf16[128,16,256]{2,1,0:T(8,128)(2,1)}), bf16[128,16,256]{2,1,0:T(8,128)(2,1)S(1)}, u32[]{:S(2)}, u32[]{:S(2)}) async-start(bf16[128,16,256]{2,1,0:T(8,128)(2,1)} %copy.32), calls=%async_computation | async-start | bytes 2097152 | tf_op jit(solution)/shard_map/all_to_all | solution.py:52
  99.3 1.2 copy-start.1
  122.6 0.7 copy-start.3
  122.6 0.7 copy-start.4
  123.3 0.8 copy-start.7
Sparse Core Ops, SparseCore 0:
  8.9 23.9 all-gather.1
where the time goes:
time: 133 us
  waiting for transfers between devices  62.6 us (47%)
  blocking collectives  26.7 us (20%)
  between operations  13.6 us (10%)
  starting transfers between devices  12.5 us (9%)
  local copies, waits for them, and re-layouts  9.62 us (7%)
  matrix products  3.78 us (3%)
  other arithmetic  3.76 us (3%)
    all_to_all x1, waiting for transfers between devices, body(): lax.all_to_all(left_edges, 'res', split_axis=0, concat_axis=1, tiled=True)  21.8 us
    all_to_all x1, blocking collectives, body(): lax.all_to_all(product.astype(jnp.bfloat16), 'res', split_axis=1, concat_...  21.1 us
    all_gather x1, waiting for transfers between devices, body(): lax.all_gather(pair, 'chan', axis=0, tiled=True)  20.1 us
    all_to_all x1, waiting for transfers between devices, body(): lax.all_to_all(right_edges, 'res', split_axis=0, concat_axis=1, tiled=True)  19.9 us
    all_to_all x1, starting transfers between devices, body(): lax.all_to_all(left_edges, 'res', split_axis=0, concat_axis=1, tiled=True)  6.86 us
    all_to_all x1, starting transfers between devices, body(): lax.all_to_all(right_edges, 'res', split_axis=0, concat_axis=1, tiled=True)  5.62 us
    all_gather x1, blocking collectives, body(): lax.all_gather(pair_mask, 'chan', axis=1, tiled=True)  5.54 us
    convert_element_type x2, local copies, waits for them, and re-layouts, edge_half(): return (jax.nn.sigmoid(gate_part) * value_part * maskf).astype(jnp.bfloat16)  3.43 us
  transfers between devices with their start and end apart: 3, of which 3 were waited for; matrix products, arithmetic and copies ran while one was open for 3% of the time, Pallas kernels for 0%

commit v1 on v0

--- a/solution.py
+++ b/solution.py
@@ -1,9 +1,17 @@
+import functools
+
 import jax
 import jax.numpy as jnp
 from jax import lax
+from jax.experimental import pallas as pl
+from jax.experimental.pallas import tpu as pltpu
 from jax.sharding import PartitionSpec as P
 
 epsilon = 1e-05
+MESH = pl.DeviceIdType.MESH
+PLANE_ROWS = 4
+CHUNKS = 4
+VMEM_LIMIT = 48 * 1024 * 1024
 
 
 def layer_norm(values, scale_gain, shift_bias):
@@ -38,7 +46,15 @@
     return (edge_half(0), edge_half(2 * hidden))
 
 
-def body(pair, pair_mask, norm_gain, norm_bias, w_edges, w_gate, out_gain, out_bias, w_out):
+def finish(normed, product_normed, w_gate, w_out):
+    gate_values = jax.nn.sigmoid(
+        jnp.einsum("cij,cd->dij", normed, w_gate, preferred_element_type=jnp.float32)
+    )
+    mixed_out = jnp.einsum("hij,hd->dij", product_normed, w_out, preferred_element_type=jnp.float32)
+    return (gate_values * mixed_out).astype(jnp.bfloat16)
+
+
+def wide_body(pair, pair_mask, norm_gain, norm_bias, w_edges, w_gate, out_gain, out_bias, w_out):
     quarter = pair_mask.shape[1]
     whole_rows, mask_rows = (
         lax.all_gather(pair, "chan", axis=0, tiled=True),
@@ -62,17 +78,349 @@
     returned = lax.all_to_all(
         product.astype(jnp.bfloat16), "res", split_axis=1, concat_axis=0, tiled=True
     )
-    gate_values = jax.nn.sigmoid(
-        jnp.einsum("cij,cd->dij", normed, w_gate, preferred_element_type=jnp.float32)
-    )
     product_normed = layer_norm(returned.astype(jnp.float32), out_gain, out_bias).astype(
         jnp.bfloat16
     )
-    mixed_out = jnp.einsum("hij,hd->dij", product_normed, w_out, preferred_element_type=jnp.float32)
-    return (gate_values * mixed_out).astype(jnp.bfloat16)
+    return finish(normed, product_normed, w_gate, w_out)
+
+
+def norm_into(source_ref, gain_ref, bias_ref, target_ref):
+    values = source_ref[...].astype(jnp.float32)
+    average = jnp.mean(values, axis=0, keepdims=True)
+    centered = values - average
+    variance = jnp.mean(centered * centered, axis=0, keepdims=True)
+    scaled = centered * lax.rsqrt(variance + epsilon)
+    target_ref[...] = (scaled * gain_ref[...] + bias_ref[...]).astype(target_ref.dtype)
+
+
+def exchange_kernel(pair_ref, gain_ref, bias_ref, normed_ref, whole, local_sem, send_sem, recv_sem):
+    groups, res, x = lax.axis_index("groups"), lax.axis_index("res"), lax.axis_index("chan")
+    other = 1 - x
+    half, _, width = pair_ref.shape
+    cols = width // 2
+    barrier = pltpu.get_barrier_semaphore()
+    pl.semaphore_signal(barrier, inc=1, device_id=(groups, res, other), device_id_type=MESH)
+    pl.semaphore_wait(barrier, 1)
+    place = whole.at[pl.ds(x * half, half)]
+    copy = pltpu.make_async_remote_copy(
+        src_ref=pair_ref.at[:, :, pl.ds(pl.multiple_of(other * cols, cols), cols)],
+        dst_ref=place,
+        send_sem=send_sem,
+        recv_sem=recv_sem,
+        device_id=(groups, res, other),
+        device_id_type=MESH,
+    )
+    copy.start()
+    local = pltpu.make_async_copy(
+        pair_ref.at[:, :, pl.ds(pl.multiple_of(x * cols, cols), cols)], place, local_sem
+    )
+    local.start()
+    local.wait()
+    copy.wait()
+    norm_into(whole, gain_ref, bias_ref, normed_ref)
+
+
+def triangle_kernel(
+    depth,
+    left_ref,
+    right_ref,
+    gain_ref,
+    bias_ref,
+    out_ref,
+    lefts,
+    rights,
+    products,
+    returned,
+    local_sem,
+    right_send,
+    right_recv,
+    left_send,
+    left_recv,
+    up_send,
+    up_recv,
+    down_send,
+    down_recv,
+    back_send,
+    back_recv,
+):
+    groups, res, x = lax.axis_index("groups"), lax.axis_index("res"), lax.axis_index("chan")
+    z, r = res // PLANE_ROWS, res % PLANE_ROWS
+    plane = 2 * PLANE_ROWS
+    p = r * 2 + x
+    rows, cols = left_ref.shape[1], left_ref.shape[2]
+    mine = left_ref.shape[0] // plane
+    step = mine // CHUNKS
+    tall = PLANE_ROWS * rows
+
+    def device(q):
+        return (groups, z * PLANE_ROWS + q // 2, q % 2)
+
+    def peer(offset):
+        return (p + offset) % plane
+
+    barrier = pltpu.get_barrier_semaphore()
+
+    def greet(offset, carry):
+        pl.semaphore_signal(barrier, inc=1, device_id=device(peer(offset)), device_id_type=MESH)
+        return carry
+
+    lax.fori_loop(1, plane, greet, 0)
+
+    @pl.when(z < depth - 1)
+    def _():
+        pl.semaphore_signal(
+            barrier, inc=1, device_id=(groups, res + PLANE_ROWS, x), device_id_type=MESH
+        )
+
+    @pl.when(z > 0)
+    def _():
+        pl.semaphore_signal(
+            barrier, inc=1, device_id=(groups, res - PLANE_ROWS, x), device_id_type=MESH
+        )
+
+    beside = jnp.where(z < depth - 1, 1, 0) + jnp.where(z > 0, 1, 0)
+    pl.semaphore_wait(barrier, plane - 1 + beside)
+
+    here = pl.ds(pl.multiple_of(z * tall + r * rows, rows), rows)
+    here_left = pl.ds(pl.multiple_of(r * rows, rows), rows)
+    here_cols = pl.ds(pl.multiple_of(x * cols, cols), cols)
+
+    def right_copy(offset, c):
+        q = peer(offset)
+        return pltpu.make_async_remote_copy(
+            src_ref=right_ref.at[pl.ds(q * mine + c * step, step)],
+            dst_ref=rights.at[pl.ds(c * step, step), here, here_cols],
+            send_sem=right_send.at[offset, c],
+            recv_sem=right_recv.at[offset, c],
+            device_id=device(q),
+            device_id_type=MESH,
+        )
+
+    def left_copy(offset):
+        q = peer(offset)
+        return pltpu.make_async_remote_copy(
+            src_ref=left_ref.at[pl.ds(q * mine, mine)],
+            dst_ref=lefts.at[:, here_left, here_cols],
+            send_sem=left_send.at[offset],
+            recv_sem=left_recv.at[offset],
+            device_id=device(q),
+            device_id_type=MESH,
+        )
+
+    own_right = pltpu.make_async_copy(
+        right_ref.at[pl.ds(p * mine, mine)], rights.at[:, here, here_cols], local_sem.at[0]
+    )
+    own_left = pltpu.make_async_copy(
+        left_ref.at[pl.ds(p * mine, mine)], lefts.at[:, here_left, here_cols], local_sem.at[1]
+    )
+    own_right.start()
+
+    def over_peers(act):
+        def one(offset, carry):
+            act(offset)
+            return carry
+
+        lax.fori_loop(1, plane, one, 0)
+
+    for c in range(CHUNKS):
+        over_peers(lambda offset: right_copy(offset, c).start())
+    own_left.start()
+    over_peers(lambda offset: left_copy(offset).start())
+
+    def hop(owner, c, upward, distance):
+        block = rights.at[
+            pl.ds(c * step, step), pl.ds(pl.multiple_of(owner * tall, tall), tall), :
+        ]
+        send, recv = (up_send, up_recv) if upward else (down_send, down_recv)
+        return pltpu.make_async_remote_copy(
+            src_ref=block,
+            dst_ref=block,
+            send_sem=send.at[distance, c],
+            recv_sem=recv.at[distance, c],
+            device_id=(groups, res + PLANE_ROWS if upward else res - PLANE_ROWS, x),
+            device_id_type=MESH,
+        )
+
+    own_right.wait()
+    for c in range(CHUNKS):
+        over_peers(lambda offset: right_copy(offset, c).wait_recv())
+
+        @pl.when(z < depth - 1)
+        def _():
+            hop(z, c, True, 0).start()
+
+        @pl.when(z > 0)
+        def _():
+            hop(z, c, False, 0).start()
+
+    def pass_on(distance, c):
+        @pl.when(z >= distance)
+        def _():
+            hop(z - distance, c, True, distance - 1).wait_recv()
+
+        @pl.when((z >= distance) & (z < depth - 1))
+        def _():
+            hop(z - distance, c, True, distance).start()
+
+        @pl.when(z + distance < depth)
+        def _():
+            hop(z + distance, c, False, distance - 1).wait_recv()
+
+        @pl.when((z + distance < depth) & (z > 0))
+        def _():
+            hop(z + distance, c, False, distance).start()
+
+    near = z // (depth // 2)
+
+    def back_copy(r_to, side, c):
+        q = r_to * 2 + side
+        offset = (q - p + plane) % plane
+        return pltpu.make_async_remote_copy(
+            src_ref=products.at[
+                side, pl.ds(c * step, step), pl.ds(pl.multiple_of(r_to * rows, rows), rows), :
+            ],
+            dst_ref=returned.at[pl.ds(p * mine + c * step, step)],
+            send_sem=back_send.at[offset, c],
+            recv_sem=back_recv.at[offset, c],
+            device_id=device(q),
+            device_id_type=MESH,
+        )
+
+    def multiply(side, c):
+        channels = pl.ds(c * step, step)
+        result = lax.dot_general(
+            lefts[channels],
+            rights[channels, pl.ds(pl.multiple_of(side * cols, cols), cols), :],
+            (((2,), (2,)), ((0,), (0,))),
+            preferred_element_type=jnp.float32,
+        )
+        products[side, channels] = result.astype(products.dtype)
+
+        def give(r_to, carry):
+            @pl.when(r_to * 2 + side != p)
+            def _():
+                back_copy(r_to, side, c).start()
+
+            return carry
+
+        lax.fori_loop(0, PLANE_ROWS, give, 0)
+
+    for c in range(CHUNKS):
+        pass_on(1, c)
+    own_left.wait()
+    over_peers(lambda offset: left_copy(offset).wait_recv())
+    for c in range(CHUNKS):
+        multiply(near, c)
+    for c in range(CHUNKS):
+        for distance in range(2, depth):
+            pass_on(distance, c)
+        multiply(1 - near, c)
+
+    own_back = pltpu.make_async_copy(
+        products.at[x, :, here_left, :], returned.at[pl.ds(p * mine, mine)], local_sem.at[2]
+    )
+    own_back.start()
+    own_back.wait()
+
+    def back_wait(offset, c, receive):
+        q = peer(offset)
+        copy = back_copy(q // 2, q % 2, c)
+        if receive:
+            copy.wait_recv()
+        else:
+            copy.wait_send()
+
+    for c in range(CHUNKS):
+        over_peers(lambda offset: back_wait(offset, c, True))
+    norm_into(returned, gain_ref, bias_ref, out_ref)
+
+    for c in range(CHUNKS):
+        over_peers(lambda offset: back_wait(offset, c, False))
+        over_peers(lambda offset: right_copy(offset, c).wait_send())
+        for distance in range(depth - 1):
+
+            @pl.when((z >= distance) & (z < depth - 1))
+            def _():
+                hop(z - distance, c, True, distance).wait_send()
+
+            @pl.when((z + distance < depth) & (z > 0))
+            def _():
+                hop(z + distance, c, False, distance).wait_send()
+
+    over_peers(lambda offset: left_copy(offset).wait_send())
+
+
+def vmem():
+    return pl.BlockSpec(memory_space=pltpu.VMEM)
+
+
+def plane_body(
+    depth, pair, pair_mask, norm_gain, norm_bias, w_edges, w_gate, out_gain, out_bias, w_out
+):
+    rows, cols = pair_mask.shape
+    channels, hidden = w_gate.shape[0], w_out.shape[0]
+    width = 2 * cols
+    plane = 2 * PLANE_ROWS
+    mine = hidden // plane
+    tall = PLANE_ROWS * rows
+    dma = pltpu.SemaphoreType.DMA
+
+    def spread(values):
+        return values[:, None, None]
+
+    normed = pl.pallas_call(
+        exchange_kernel,
+        out_shape=jax.ShapeDtypeStruct((channels, rows, cols), jnp.bfloat16),
+        in_specs=[pl.BlockSpec(memory_space=pl.ANY), vmem(), vmem()],
+        out_specs=vmem(),
+        scratch_shapes=[
+            pltpu.VMEM((channels, rows, cols), jnp.bfloat16),
+            dma(()),
+            dma(()),
+            dma(()),
+        ],
+        compiler_params=pltpu.CompilerParams(
+            collective_id=0, has_side_effects=True, vmem_limit_bytes=VMEM_LIMIT
+        ),
+        name="exchange",
+    )(pair, spread(norm_gain), spread(norm_bias))
+    left_edges, right_edges = project_edges(normed, pair_mask, w_edges)
+    product_normed = pl.pallas_call(
+        functools.partial(triangle_kernel, depth),
+        out_shape=jax.ShapeDtypeStruct((hidden, rows, cols), jnp.bfloat16),
+        in_specs=[vmem()] * 4,
+        out_specs=vmem(),
+        scratch_shapes=[
+            pltpu.VMEM((mine, tall, width), jnp.bfloat16),
+            pltpu.VMEM((mine, depth * tall, width), jnp.bfloat16),
+            pltpu.VMEM((2, mine, tall, cols), jnp.bfloat16),
+            pltpu.VMEM((hidden, rows, cols), jnp.bfloat16),
+            dma((3,)),
+            dma((plane, CHUNKS)),
+            dma((plane, CHUNKS)),
+            dma((plane,)),
+            dma((plane,)),
+            dma((depth - 1, CHUNKS)),
+            dma((depth - 1, CHUNKS)),
+            dma((depth - 1, CHUNKS)),
+            dma((depth - 1, CHUNKS)),
+            dma((plane, CHUNKS)),
+            dma((plane, CHUNKS)),
+        ],
+        compiler_params=pltpu.CompilerParams(
+            collective_id=1, has_side_effects=True, vmem_limit_bytes=VMEM_LIMIT
+        ),
+        name="triangle",
+    )(left_edges, right_edges, spread(out_gain), spread(out_bias))
+    return finish(normed, product_normed, w_gate, w_out)
 
 
 def solution(mesh):
+    sizes = dict(mesh.shape)
+    depth = sizes["res"] // PLANE_ROWS
+    body = wide_body
+    if sizes["chan"] == 2 and sizes["res"] % PLANE_ROWS == 0 and depth in (2, 4):
+        body = functools.partial(plane_body, depth)
     return jax.shard_map(
         body,
         mesh=mesh,

time: 133 us -> 77 us (0.58)
  the two profiles are of different devices: /device:TPU:0 before, /device:TPU:25 now
where the time goes in v1:
time: 77 us; the launch traced here: 75.9 us
  Pallas kernels  57.4 us (75%)
  local copies, waits for them, and re-layouts  12.2 us (16%)
  other arithmetic  3.49 us (5%)
  matrix products  2.66 us (3%)
    pallas_call x1, Pallas kernels, plane_body(): pl.pallas_call(functools.partial(triangle_kernel, depth), out_shape=jax.S...  49.7 us
    pallas_call x1, Pallas kernels, plane_body(): pl.pallas_call(exchange_kernel, out_shape=jax.ShapeDtypeStruct((channels,...  7.7 us
    unnamed x18, local copies, waits for them, and re-layouts  4.33 us
    dot_general x2, local copies, waits for them, and re-layouts, edge_half(): jnp.einsum('cij,ch->hij', normed, w_edges[:, offset + hidden:offset + 2 *...  2.76 us
    convert_element_type x1, other arithmetic, edge_half(): return (jax.nn.sigmoid(gate_part) * value_part * maskf).astype(jnp.bfloat16)  2.41 us
    dot_general x2, local copies, waits for them, and re-layouts, edge_half(): jnp.einsum('cij,ch->hij', normed, w_edges[:, offset:offset + hidden], pre...  1.94 us
    dot_general x1, local copies, waits for them, and re-layouts, finish(): jnp.einsum('cij,cd->dij', normed, w_gate, preferred_element_type=jnp.floa...  1.73 us

profile of v1, /device:TPU:25, one launch (start us, length us, event | category | flops | bytes accessed | tf_op | source)
XLA Modules:
  0.0 75.9 jit_solution(2244421206980658762)
XLA Ops:
  0.0 0.7 copy-done.5
  0.7 0.1 copy.10.gain_ref
  0.8 0.7 copy-done.6
  1.4 0.1 copy.11.bias_ref
  1.6 1.0 %copy-done.1 = bf16[64,16,256]{2,1,0:T(8,128)(2,1)S(1)} copy-done((bf16[64,16,256]{2,1,0:T(8,128)(2,1)S(1)}, bf16[64,16,256]{2,1,0:T(8,128)(2,1)}, u32[]{:S(2)}) %copy-start.1) | copy-done | bytes 524312
  2.6 7.7 %exchange.1 = bf16[128,16,128]{2,1,0:T(8,128)(2,1)S(1)} custom-call(bf16[64,16,256]{2,1,0:T(8,128)(2,1)S(1)} %copy-done.1, f32[128,1,1]{2,1,0:T(1,128)S(1)} %copy.10.gain_ref, f32[128,1,1]{2,1,0:T(1,128)S(1)} %copy.11.bias_ref), custom_call_target="tpu_custom_call" | custom-call | tf_op jit(solution)/shard_map/exchange/pallas_call | solution.py:371
  10.3 0.0 copy-start.2
  10.3 0.5 copy.12
  10.8 0.4 copy-done.2
  11.2 0.3 fusion.12
  11.5 0.5 copy.18
  12.0 0.3 fusion.10
  12.3 1.4 %copy.19 = f32[16,128,128]{1,0,2:T(8,128)} copy(f32[16,128,128]{2,1,0:T(8,128)S(1)} %fusion.10) | data formatting | bytes 2097152 | tf_op jit(solution)/shard_map/cij,ch->hij/dot_general | solution.py:38
  13.7 0.3 fusion.8
  13.9 1.4 %copy.20 = f32[16,128,128]{1,0,2:T(8,128)} copy(f32[16,128,128]{2,1,0:T(8,128)S(1)} %fusion.8) | data formatting | bytes 2097152 | tf_op jit(solution)/shard_map/cij,ch->hij/dot_general | solution.py:32
  15.4 0.3 fusion.6
  15.6 0.0 copy-start.4
  15.7 1.4 %copy.21 = f32[16,128,128]{1,0,2:T(8,128)} copy(f32[16,128,128]{2,1,0:T(8,128)S(1)} %fusion.6) | data formatting | bytes 2097152 | tf_op jit(solution)/shard_map/cij,ch->hij/dot_general | solution.py:38
  17.0 2.4 %fusion.4 = (bf16[128,16,128]{2,1,0:T(8,128)(2,1)S(1)}, bf16[128,16,128]{2,1,0:T(8,128)(2,1)S(1)}) fusion(f32[16,128]{1,0:T(8,128)S(1)} %convert_element_type.12, f32[16,128,128]{1,0,2:T(8,128)} %copy.21, f32[16,128,128]{1,0,2:T(8,128)} %copy.20, f32[16,128,128]{1,0,2:T(8,128)} %copy.19, f32[16,128,128]{1,0,2:T(8,128)S(1)} %copy.18), kind=kLoop, calls=%fused_computation.7 | loop fusion | flops 3145728 | bytes 5251072 | tf_op jit(solution)/shard_map/convert_element_type | solution.py:44
  19.4 0.0 copy-start.7
  19.5 0.6 copy-done.7
  20.1 0.1 copy.14.gain_ref
  20.2 0.7 copy-done.8
  20.9 0.1 copy.15.bias_ref
  21.0 49.7 %triangle.1 = bf16[128,16,128]{2,1,0:T(8,128)(2,1)S(1)} custom-call(bf16[128,16,128]{2,1,0:T(8,128)(2,1)S(1)} %get-tuple-element.6.left_ref, bf16[128,16,128]{2,1,0:T(8,128)(2,1)S(1)} %get-tuple-element.5.right_ref, f32[128,1,1]{2,1,0:T(1,128)S(1)} %copy.14.gain_ref, f32[128,1,1]{2,1,0:T(1,128)S(1)} %copy.15.bias_ref), custom_call_target="tpu_custom_call" | custom-call | tf_op jit(solution)/shard_map/triangle/pallas_call | solution.py:388
  70.7 0.3 fusion
  71.0 0.0 copy-start.3
  71.1 0.5 copy.17
  71.6 0.2 copy-done.3
  71.8 1.2 %fusion.14 = f32[16,128,128]{2,1,0:T(8,128)} fusion(bf16[128,16,128]{0,2,1:T(8,128)(2,1)S(1)} %copy.12, bf16[128,128]{1,0:T(8,128)(2,1)S(1)} %copy-done.3), kind=kOutput, calls=%fused_computation.17 | convolution fusion | flops 67108864 | bytes 1605632 | tf_op jit(solution)/shard_map/cij,cd->dij/dot_general | solution.py:51
  73.0 1.7 %copy.13 = f32[16,128,128]{1,0,2:T(8,128)S(1)} copy(f32[16,128,128]{2,1,0:T(8,128)} %fusion.14) | data formatting | bytes 2097152 | tf_op jit(solution)/shard_map/cij,cd->dij/dot_general | solution.py:51
  74.8 1.1 %fusion.2 = bf16[128,16,128]{2,1,0:T(8,128)(2,1)} fusion(f32[16,128,128]{1,0,2:T(8,128)S(1)} %copy.17, f32[16,128,128]{1,0,2:T(8,128)S(1)} %copy.13), kind=kLoop, calls=%fused_computation.5 | loop fusion | flops 1310720 | bytes 2621440 | tf_op jit(solution)/shard_map/convert_element_type | solution.py:54
  (8 shorter events, 0.0 us)
Async XLA Ops:
  0.0 70.7 %copy-start = (bf16[128,128]{1,0:T(8,128)(2,1)S(1)}, bf16[128,128]{1,0:T(8,128)(2,1)}, u32[]{:S(2)}) copy-start(bf16[128,128]{1,0:T(8,128)(2,1)} %param.17) | copy-start | bytes 98308
  0.0 0.7 copy-start.5
  0.8 0.7 copy-start.6
  1.5 1.0 %copy-start.1 = (bf16[64,16,256]{2,1,0:T(8,128)(2,1)S(1)}, bf16[64,16,256]{2,1,0:T(8,128)(2,1)}, u32[]{:S(2)}) copy-start(bf16[64,16,256]{2,1,0:T(8,128)(2,1)} %pair_ref.1) | copy-start | bytes 1572868
  10.3 0.9 %copy-start.2 = (bf16[128,512]{1,0:T(8,128)(2,1)S(1)}, bf16[128,512]{1,0:T(8,128)(2,1)}, u32[]{:S(2)}) copy-start(bf16[128,512]{1,0:T(8,128)(2,1)} %param.13) | copy-start | bytes 393220
  15.6 1.4 %copy-start.4 = (s32[16,128]{1,0:T(8,128)S(1)}, s32[16,128]{1,0:T(8,128)}, u32[]{:S(2)}) copy-start(s32[16,128]{1,0:T(8,128)} %param.10) | copy-start | bytes 24580
  19.4 0.7 copy-start.7
  20.2 0.7 copy-start.8
  71.0 0.8 %copy-start.3 = (bf16[128,128]{1,0:T(8,128)(2,1)S(1)}, bf16[128,128]{1,0:T(8,128)(2,1)}, u32[]{:S(2)}) copy-start(bf16[128,128]{1,0:T(8,128)(2,1)} %param.14) | copy-start | bytes 98308

commit v2 on v1

--- a/solution.py
+++ b/solution.py
@@ -11,6 +11,7 @@
 MESH = pl.DeviceIdType.MESH
 PLANE_ROWS = 4
 CHUNKS = 4
+UNROLL = 2
 VMEM_LIMIT = 48 * 1024 * 1024
 
 
@@ -84,54 +85,47 @@
     return finish(normed, product_normed, w_gate, w_out)
 
 
-def norm_into(source_ref, gain_ref, bias_ref, target_ref):
-    values = source_ref[...].astype(jnp.float32)
+def centre(source):
+    values = source.astype(jnp.float32)
     average = jnp.mean(values, axis=0, keepdims=True)
     centered = values - average
     variance = jnp.mean(centered * centered, axis=0, keepdims=True)
-    scaled = centered * lax.rsqrt(variance + epsilon)
-    target_ref[...] = (scaled * gain_ref[...] + bias_ref[...]).astype(target_ref.dtype)
-
-
-def exchange_kernel(pair_ref, gain_ref, bias_ref, normed_ref, whole, local_sem, send_sem, recv_sem):
-    groups, res, x = lax.axis_index("groups"), lax.axis_index("res"), lax.axis_index("chan")
-    other = 1 - x
-    half, _, width = pair_ref.shape
-    cols = width // 2
-    barrier = pltpu.get_barrier_semaphore()
-    pl.semaphore_signal(barrier, inc=1, device_id=(groups, res, other), device_id_type=MESH)
-    pl.semaphore_wait(barrier, 1)
-    place = whole.at[pl.ds(x * half, half)]
-    copy = pltpu.make_async_remote_copy(
-        src_ref=pair_ref.at[:, :, pl.ds(pl.multiple_of(other * cols, cols), cols)],
-        dst_ref=place,
-        send_sem=send_sem,
-        recv_sem=recv_sem,
-        device_id=(groups, res, other),
-        device_id_type=MESH,
-    )
-    copy.start()
-    local = pltpu.make_async_copy(
-        pair_ref.at[:, :, pl.ds(pl.multiple_of(x * cols, cols), cols)], place, local_sem
-    )
-    local.start()
-    local.wait()
-    copy.wait()
-    norm_into(whole, gain_ref, bias_ref, normed_ref)
+    return centered * lax.rsqrt(variance + epsilon)
 
 
 def triangle_kernel(
     depth,
+    pair_ref,
+    mask_ref,
+    columns_ref,
+    edges_ref,
+    gate_ref,
+    last_ref,
+    out_ref,
+    whole,
+    mask,
+    columns,
+    edges,
+    gate_weight,
+    last_weight,
+    edges_t,
+    gate_t,
+    last_t,
+    wide,
+    scaled,
+    staged,
+    normed,
+    gates,
     left_ref,
     right_ref,
-    gain_ref,
-    bias_ref,
-    out_ref,
     lefts,
     rights,
     products,
     returned,
     local_sem,
+    load_sem,
+    pair_send,
+    pair_recv,
     right_send,
     right_recv,
     left_send,
@@ -148,9 +142,31 @@
     plane = 2 * PLANE_ROWS
     p = r * 2 + x
     rows, cols = left_ref.shape[1], left_ref.shape[2]
+    half = pair_ref.shape[0]
+    channels, hidden = normed.shape[1], left_ref.shape[0]
     mine = left_ref.shape[0] // plane
     step = mine // CHUNKS
     tall = PLANE_ROWS * rows
+
+    loads = [
+        pltpu.make_async_copy(source, target, load_sem.at[index])
+        for index, (source, target) in enumerate(
+            (
+                (columns_ref, columns),
+                (edges_ref, edges),
+                (gate_ref, gate_weight),
+                (last_ref, last_weight),
+                (mask_ref, mask),
+            )
+        )
+    ]
+    place = whole.at[pl.ds(x * half, half)]
+    own_pair = pltpu.make_async_copy(
+        pair_ref.at[:, :, pl.ds(pl.multiple_of(x * cols, cols), cols)], place, local_sem.at[3]
+    )
+    own_pair.start()
+    for load in loads:
+        load.start()
 
     def device(q):
         return (groups, z * PLANE_ROWS + q // 2, q % 2)
@@ -180,6 +196,56 @@
 
     beside = jnp.where(z < depth - 1, 1, 0) + jnp.where(z > 0, 1, 0)
     pl.semaphore_wait(barrier, plane - 1 + beside)
+
+    other = 1 - x
+    swap = pltpu.make_async_remote_copy(
+        src_ref=pair_ref.at[:, :, pl.ds(pl.multiple_of(other * cols, cols), cols)],
+        dst_ref=place,
+        send_sem=pair_send,
+        recv_sem=pair_recv,
+        device_id=(groups, res, other),
+        device_id_type=MESH,
+    )
+    swap.start()
+    for load in loads:
+        load.wait()
+    for index in range(4):
+        wide[index] = jnp.broadcast_to(columns[:, index : index + 1], wide.shape[1:])
+    edges_t[...] = edges[...].T
+    gate_t[...] = gate_weight[...].T
+    last_t[...] = last_weight[...].T
+    own_pair.wait()
+    swap.wait_recv()
+    scaled[...] = centre(whole[...]).reshape(scaled.shape)
+
+    def line(i, count):
+        return pl.ds(i, count, stride=rows)
+
+    def project(i, offset):
+        parts = jnp.dot(
+            edges_t[offset : offset + 2 * hidden, :], normed[i], preferred_element_type=jnp.float32
+        )
+        valid = mask[pl.ds(i, 1), :].astype(jnp.float32)
+        staged[line(i, hidden), :] = jax.nn.sigmoid(parts[:hidden]) * parts[hidden:] * valid
+
+    def right_row(i, carry):
+        values = scaled[line(i, channels), :] * wide[0] + wide[1]
+        normed[i] = values.astype(normed.dtype)
+        project(i, 2 * hidden)
+        return carry
+
+    def left_row(i, carry):
+        project(i, 0)
+        return carry
+
+    def gate_row(i, carry):
+        gates[i] = jax.nn.sigmoid(
+            jnp.dot(gate_t[...], normed[i], preferred_element_type=jnp.float32)
+        )
+        return carry
+
+    lax.fori_loop(0, rows, right_row, 0, unroll=UNROLL)
+    right_ref[...] = staged[...].reshape(right_ref.shape).astype(right_ref.dtype)
 
     here = pl.ds(pl.multiple_of(z * tall + r * rows, rows), rows)
     here_left = pl.ds(pl.multiple_of(r * rows, rows), rows)
@@ -224,6 +290,8 @@
 
     for c in range(CHUNKS):
         over_peers(lambda offset: right_copy(offset, c).start())
+    lax.fori_loop(0, rows, left_row, 0, unroll=UNROLL)
+    left_ref[...] = staged[...].reshape(left_ref.shape).astype(left_ref.dtype)
     own_left.start()
     over_peers(lambda offset: left_copy(offset).start())
 
@@ -253,6 +321,8 @@
         def _():
             hop(z, c, False, 0).start()
 
+    lax.fori_loop(0, rows, gate_row, 0, unroll=UNROLL)
+
     def pass_on(distance, c):
         @pl.when(z >= distance)
         def _():
@@ -287,14 +357,14 @@
         )
 
     def multiply(side, c):
-        channels = pl.ds(c * step, step)
+        part = pl.ds(c * step, step)
         result = lax.dot_general(
-            lefts[channels],
-            rights[channels, pl.ds(pl.multiple_of(side * cols, cols), cols), :],
+            lefts[part],
+            rights[part, pl.ds(pl.multiple_of(side * cols, cols), cols), :],
             (((2,), (2,)), ((0,), (0,))),
             preferred_element_type=jnp.float32,
         )
-        products[side, channels] = result.astype(products.dtype)
+        products[side, part] = result.astype(products.dtype)
 
         def give(r_to, carry):
             @pl.when(r_to * 2 + side != p)
@@ -332,7 +402,18 @@
 
     for c in range(CHUNKS):
         over_peers(lambda offset: back_wait(offset, c, True))
-    norm_into(returned, gain_ref, bias_ref, out_ref)
+    scaled[...] = centre(returned[...]).reshape(scaled.shape)
+
+    def last_row(i, carry):
+        values = scaled[line(i, hidden), :] * wide[2] + wide[3]
+        mixed = jnp.dot(
+            last_t[...], values.astype(jnp.bfloat16), preferred_element_type=jnp.float32
+        )
+        staged[line(i, channels), :] = gates[i] * mixed
+        return carry
+
+    lax.fori_loop(0, rows, last_row, 0, unroll=UNROLL)
+    out_ref[...] = staged[...].reshape(out_ref.shape).astype(out_ref.dtype)
 
     for c in range(CHUNKS):
         over_peers(lambda offset: back_wait(offset, c, False))
@@ -348,10 +429,7 @@
                 hop(z + distance, c, False, distance).wait_send()
 
     over_peers(lambda offset: left_copy(offset).wait_send())
-
-
-def vmem():
-    return pl.BlockSpec(memory_space=pltpu.VMEM)
+    swap.wait_send()
 
 
 def plane_body(
@@ -365,37 +443,38 @@
     tall = PLANE_ROWS * rows
     dma = pltpu.SemaphoreType.DMA
 
-    def spread(values):
-        return values[:, None, None]
-
-    normed = pl.pallas_call(
-        exchange_kernel,
-        out_shape=jax.ShapeDtypeStruct((channels, rows, cols), jnp.bfloat16),
-        in_specs=[pl.BlockSpec(memory_space=pl.ANY), vmem(), vmem()],
-        out_specs=vmem(),
+    columns = jnp.stack([norm_gain, norm_bias, out_gain, out_bias], axis=1)
+    bf16, f32 = jnp.bfloat16, jnp.float32
+    return pl.pallas_call(
+        functools.partial(triangle_kernel, depth),
+        out_shape=jax.ShapeDtypeStruct((channels, rows, cols), bf16),
+        in_specs=[pl.BlockSpec(memory_space=pltpu.HBM)] * 6,
+        out_specs=pl.BlockSpec(memory_space=pltpu.VMEM),
         scratch_shapes=[
-            pltpu.VMEM((channels, rows, cols), jnp.bfloat16),
+            pltpu.VMEM((channels, rows, cols), bf16),
+            pltpu.VMEM(pair_mask.shape, pair_mask.dtype),
+            pltpu.VMEM(columns.shape, f32),
+            pltpu.VMEM(w_edges.shape, bf16),
+            pltpu.VMEM(w_gate.shape, bf16),
+            pltpu.VMEM(w_out.shape, bf16),
+            pltpu.VMEM(w_edges.shape[::-1], bf16),
+            pltpu.VMEM(w_gate.shape[::-1], bf16),
+            pltpu.VMEM(w_out.shape[::-1], bf16),
+            pltpu.VMEM((4, channels, cols), f32),
+            pltpu.VMEM((channels * rows, cols), f32),
+            pltpu.VMEM((hidden * rows, cols), f32),
+            pltpu.VMEM((rows, channels, cols), bf16),
+            pltpu.VMEM((rows, channels, cols), f32),
+            pltpu.VMEM((hidden, rows, cols), bf16),
+            pltpu.VMEM((hidden, rows, cols), bf16),
+            pltpu.VMEM((mine, tall, width), bf16),
+            pltpu.VMEM((mine, depth * tall, width), bf16),
+            pltpu.VMEM((2, mine, tall, cols), bf16),
+            pltpu.VMEM((hidden, rows, cols), bf16),
+            dma((4,)),
+            dma((5,)),
             dma(()),
             dma(()),
-            dma(()),
-        ],
-        compiler_params=pltpu.CompilerParams(
-            collective_id=0, has_side_effects=True, vmem_limit_bytes=VMEM_LIMIT
-        ),
-        name="exchange",
-    )(pair, spread(norm_gain), spread(norm_bias))
-    left_edges, right_edges = project_edges(normed, pair_mask, w_edges)
-    product_normed = pl.pallas_call(
-        functools.partial(triangle_kernel, depth),
-        out_shape=jax.ShapeDtypeStruct((hidden, rows, cols), jnp.bfloat16),
-        in_specs=[vmem()] * 4,
-        out_specs=vmem(),
-        scratch_shapes=[
-            pltpu.VMEM((mine, tall, width), jnp.bfloat16),
-            pltpu.VMEM((mine, depth * tall, width), jnp.bfloat16),
-            pltpu.VMEM((2, mine, tall, cols), jnp.bfloat16),
-            pltpu.VMEM((hidden, rows, cols), jnp.bfloat16),
-            dma((3,)),
             dma((plane, CHUNKS)),
             dma((plane, CHUNKS)),
             dma((plane,)),
@@ -411,8 +490,7 @@
             collective_id=1, has_side_effects=True, vmem_limit_bytes=VMEM_LIMIT
         ),
         name="triangle",
-    )(left_edges, right_edges, spread(out_gain), spread(out_bias))
-    return finish(normed, product_normed, w_gate, w_out)
+    )(pair, pair_mask, columns, w_edges, w_gate, w_out)
 
 
 def solution(mesh):

time: 77 us -> 66.3 us (0.86)
  local copies, waits for them, and re-layouts: 12.2 us -> 4.18 us
  Pallas kernels: 57.4 us -> 60.9 us
  other arithmetic: 3.49 us -> 0.01 us
  matrix products: 2.66 us -> 0 us
    pallas_call x1, Pallas kernels: 49.7 us -> 60.9 us  [plane_body(): pl.pallas_call(functools.partial(triangle_kernel, depth), out_shape=jax.S...]
    pallas_call x1 -> x0, Pallas kernels: 7.7 us -> none  [plane_body(): pl.pallas_call(exchange_kernel, out_shape=jax.ShapeDtypeStruct((channels,...]
    dot_general x6 -> x0, local copies, waits for them, and re-layouts: 6.93 us -> none  [the longest x2 2.76 us: edge_half(): jnp.einsum('cij,ch->hij', normed, w_edges[:, offset + hidden:offset + 2 *...]
    convert_element_type x3 -> x0, other arithmetic: 3.49 us -> none  [the longest x1 2.41 us: edge_half(): return (jax.nn.sigmoid(gate_part) * value_part * maskf).astype(jnp.bfloat16)]
    dot_general x6 -> x0, matrix products: 2.66 us -> none  [the longest x1 1.23 us: finish(): jnp.einsum('cij,cd->dij', normed, w_gate, preferred_element_type=jnp.floa...]
    unnamed x18 -> x19, local copies, waits for them, and re-layouts: 4.33 us -> 4.07 us
where the time goes in v2:
time: 66.3 us; the launch traced here: 65.1 us
  Pallas kernels  60.9 us (92%)
  local copies, waits for them, and re-layouts  4.18 us (6%)
    pallas_call x1, Pallas kernels, plane_body(): pl.pallas_call(functools.partial(triangle_kernel, depth), out_shape=jax.S...  60.9 us
    unnamed x19, local copies, waits for them, and re-layouts  4.07 us

profile of v2, /device:TPU:25, one launch (start us, length us, event | category | flops | bytes accessed | tf_op | source)
XLA Modules:
  0.0 65.1 jit_solution(10595937316975512591)
XLA Ops:
  0.0 0.0 copy-start.5
  0.0 0.0 copy-start.6
  0.0 0.0 copy-start.7
  0.0 0.0 copy-start.8
  0.0 0.0 copy-start.4
  0.0 0.6 copy-done.5
  0.7 0.0 copy-done.6
  0.7 0.0 copy-done.7
  0.7 0.0 copy-done.8
  0.7 0.0 copy-start.2
  0.7 0.0 copy-start.3
  0.7 0.1 copy.14.columns_ref
  0.9 0.0 copy-done.4
  0.9 0.6 copy-done.2
  1.5 0.0 copy-done.3
  1.5 0.0 copy-start
  1.5 1.0 %copy-done = bf16[64,16,256]{2,1,0:T(8,128)(2,1)S(1)} copy-done((bf16[64,16,256]{2,1,0:T(8,128)(2,1)S(1)}, bf16[64,16,256]{2,1,0:T(8,128)(2,1)}, u32[]{:S(2)}) %copy-start) | copy-done | bytes 524312
  2.5 0.0 copy-start.1
  2.5 0.9 %copy-done.1 = bf16[128,512]{1,0:T(8,128)(2,1)S(1)} copy-done((bf16[128,512]{1,0:T(8,128)(2,1)S(1)}, bf16[128,512]{1,0:T(8,128)(2,1)}, u32[]{:S(2)}) %copy-start.1) | copy-done | bytes 131096
  3.4 60.9 %triangle.1 = bf16[128,16,128]{2,1,0:T(8,128)(2,1)S(1)} custom-call(bf16[64,16,256]{2,1,0:T(8,128)(2,1)S(1)} %copy-done, s32[16,128]{1,0:T(8,128)S(1)} %copy-done.4, f32[128,4]{1,0:T(8,128)S(1)} %copy.14.columns_ref, bf16[128,512]{1,0:T(8,128)(2,1)S(1)} %copy-done.1, bf16[128,128]{1,0:T(8,128)(2,1)S(1)} %copy-done.2, bf16[128,128]{1,0:T(8,128)(2,1)S(1)} %copy-done.3), custom_call_target="tpu_custom_call" | custom-call | tf_op jit(solution)/shard_map/triangle/pallas_call | solution.py:448
  64.4 0.8 %copy.16 = bf16[128,16,128]{2,1,0:T(8,128)(2,1)} copy(bf16[128,16,128]{2,1,0:T(8,128)(2,1)S(1)} %triangle.1) | data formatting | bytes 1048576
  (1 shorter events, 0.0 us)
Async XLA Ops:
  0.0 0.7 %copy-start.5 = (f32[128]{0:T(128)S(1)}, f32[128]{0:T(128)}, u32[]{:S(2)}) copy-start(f32[128]{0:T(128)} %param.16) | copy-start | bytes 1540
  0.0 0.7 %copy-start.6 = (f32[128]{0:T(128)S(1)}, f32[128]{0:T(128)}, u32[]{:S(2)}) copy-start(f32[128]{0:T(128)} %param.15) | copy-start | bytes 1540
  0.0 0.7 %copy-start.7 = (f32[128]{0:T(128)S(1)}, f32[128]{0:T(128)}, u32[]{:S(2)}) copy-start(f32[128]{0:T(128)} %param.12) | copy-start | bytes 1540
  0.0 0.7 %copy-start.8 = (f32[128]{0:T(128)S(1)}, f32[128]{0:T(128)}, u32[]{:S(2)}) copy-start(f32[128]{0:T(128)} %param.11) | copy-start | bytes 1540
  0.0 0.8 %copy-start.4 = (s32[16,128]{1,0:T(8,128)S(1)}, s32[16,128]{1,0:T(8,128)}, u32[]{:S(2)}) copy-start(s32[16,128]{1,0:T(8,128)} %mask_ref.1) | copy-start | bytes 24580
  0.7 0.8 %copy-start.2 = (bf16[128,128]{1,0:T(8,128)(2,1)S(1)}, bf16[128,128]{1,0:T(8,128)(2,1)}, u32[]{:S(2)}) copy-start(bf16[128,128]{1,0:T(8,128)(2,1)} %gate_ref.1) | copy-start | bytes 98308
  0.7 0.8 %copy-start.3 = (bf16[128,128]{1,0:T(8,128)(2,1)S(1)}, bf16[128,128]{1,0:T(8,128)(2,1)}, u32[]{:S(2)}) copy-start(bf16[128,128]{1,0:T(8,128)(2,1)} %last_ref.1) | copy-start | bytes 98308
  1.5 1.0 %copy-start = (bf16[64,16,256]{2,1,0:T(8,128)(2,1)S(1)}, bf16[64,16,256]{2,1,0:T(8,128)(2,1)}, u32[]{:S(2)}) copy-start(bf16[64,16,256]{2,1,0:T(8,128)(2,1)} %pair_ref.1) | copy-start | bytes 1572868
  2.5 0.9 %copy-start.1 = (bf16[128,512]{1,0:T(8,128)(2,1)S(1)}, bf16[128,512]{1,0:T(8,128)(2,1)}, u32[]{:S(2)}) copy-start(bf16[128,512]{1,0:T(8,128)(2,1)} %edges_ref.1) | copy-start | bytes 393220

commit v3 on v2

--- a/solution.py
+++ b/solution.py
@@ -12,7 +12,7 @@
 PLANE_ROWS = 4
 CHUNKS = 4
 UNROLL = 2
-VMEM_LIMIT = 48 * 1024 * 1024
+VMEM_LIMIT = 60 * 1024 * 1024
 
 
 def layer_norm(values, scale_gain, shift_bias):
@@ -94,7 +94,6 @@
 
 
 def triangle_kernel(
-    depth,
     pair_ref,
     mask_ref,
     columns_ref,
@@ -130,10 +129,8 @@
     right_recv,
     left_send,
     left_recv,
-    up_send,
-    up_recv,
-    down_send,
-    down_recv,
+    hop_send,
+    hop_recv,
     back_send,
     back_recv,
 ):
@@ -168,34 +165,43 @@
     for load in loads:
         load.start()
 
-    def device(q):
-        return (groups, z * PLANE_ROWS + q // 2, q % 2)
+    pod = z // 2
+    hub_z, end_z = 1 + pod, 3 * pod
+    is_hub = z == hub_z
+    kind = jnp.where(is_hub, 0, 1)
+    first = jnp.where(is_hub, 1, 0)
+
+    def device(q, plane_z):
+        return (groups, plane_z * PLANE_ROWS + q // 2, q % 2)
 
     def peer(offset):
         return (p + offset) % plane
 
     barrier = pltpu.get_barrier_semaphore()
 
+    def signal(target):
+        pl.semaphore_signal(barrier, inc=1, device_id=target, device_id_type=MESH)
+
     def greet(offset, carry):
-        pl.semaphore_signal(barrier, inc=1, device_id=device(peer(offset)), device_id_type=MESH)
+        signal(device(peer(offset), hub_z))
         return carry
 
-    lax.fori_loop(1, plane, greet, 0)
-
-    @pl.when(z < depth - 1)
+    def greet_end(offset, carry):
+        signal(device(peer(offset), end_z))
+        return carry
+
+    lax.fori_loop(first, plane, greet, 0)
+
+    @pl.when(is_hub)
     def _():
-        pl.semaphore_signal(
-            barrier, inc=1, device_id=(groups, res + PLANE_ROWS, x), device_id_type=MESH
-        )
-
-    @pl.when(z > 0)
+        lax.fori_loop(0, plane, greet_end, 0)
+        signal(device(p, 3 - hub_z))
+
+    @pl.when(z == end_z)
     def _():
-        pl.semaphore_signal(
-            barrier, inc=1, device_id=(groups, res - PLANE_ROWS, x), device_id_type=MESH
-        )
-
-    beside = jnp.where(z < depth - 1, 1, 0) + jnp.where(z > 0, 1, 0)
-    pl.semaphore_wait(barrier, plane - 1 + beside)
+        signal((groups, res, 1 - x))
+
+    pl.semaphore_wait(barrier, jnp.where(is_hub, 2 * plane, plane + 1))
 
     other = 1 - x
     swap = pltpu.make_async_remote_copy(
@@ -251,25 +257,25 @@
     here_left = pl.ds(pl.multiple_of(r * rows, rows), rows)
     here_cols = pl.ds(pl.multiple_of(x * cols, cols), cols)
 
-    def right_copy(offset, c):
+    def right_copy(offset, c, sender):
         q = peer(offset)
         return pltpu.make_async_remote_copy(
             src_ref=right_ref.at[pl.ds(q * mine + c * step, step)],
             dst_ref=rights.at[pl.ds(c * step, step), here, here_cols],
             send_sem=right_send.at[offset, c],
-            recv_sem=right_recv.at[offset, c],
-            device_id=device(q),
+            recv_sem=right_recv.at[sender, offset, c],
+            device_id=device(q, hub_z),
             device_id_type=MESH,
         )
 
-    def left_copy(offset):
+    def left_copy(offset, sender):
         q = peer(offset)
         return pltpu.make_async_remote_copy(
             src_ref=left_ref.at[pl.ds(q * mine, mine)],
-            dst_ref=lefts.at[:, here_left, here_cols],
+            dst_ref=lefts.at[kind, :, here_left, here_cols],
             send_sem=left_send.at[offset],
-            recv_sem=left_recv.at[offset],
-            device_id=device(q),
+            recv_sem=left_recv.at[sender, offset],
+            device_id=device(q, hub_z),
             device_id_type=MESH,
         )
 
@@ -277,131 +283,121 @@
         right_ref.at[pl.ds(p * mine, mine)], rights.at[:, here, here_cols], local_sem.at[0]
     )
     own_left = pltpu.make_async_copy(
-        left_ref.at[pl.ds(p * mine, mine)], lefts.at[:, here_left, here_cols], local_sem.at[1]
-    )
-    own_right.start()
-
-    def over_peers(act):
+        left_ref.at[pl.ds(p * mine, mine)], lefts.at[0, :, here_left, here_cols], local_sem.at[1]
+    )
+
+    def over_peers(start, act):
         def one(offset, carry):
             act(offset)
             return carry
 
-        lax.fori_loop(1, plane, one, 0)
+        lax.fori_loop(start, plane, one, 0)
 
     for c in range(CHUNKS):
-        over_peers(lambda offset: right_copy(offset, c).start())
+        over_peers(first, lambda offset: right_copy(offset, c, kind).start())
+
+    @pl.when(is_hub)
+    def _():
+        own_right.start()
+
     lax.fori_loop(0, rows, left_row, 0, unroll=UNROLL)
     left_ref[...] = staged[...].reshape(left_ref.shape).astype(left_ref.dtype)
-    own_left.start()
-    over_peers(lambda offset: left_copy(offset).start())
-
-    def hop(owner, c, upward, distance):
+    over_peers(first, lambda offset: left_copy(offset, kind).start())
+
+    def hop(owner, c, sender):
         block = rights.at[
             pl.ds(c * step, step), pl.ds(pl.multiple_of(owner * tall, tall), tall), :
         ]
-        send, recv = (up_send, up_recv) if upward else (down_send, down_recv)
         return pltpu.make_async_remote_copy(
             src_ref=block,
             dst_ref=block,
-            send_sem=send.at[distance, c],
-            recv_sem=recv.at[distance, c],
-            device_id=(groups, res + PLANE_ROWS if upward else res - PLANE_ROWS, x),
+            send_sem=hop_send.at[sender, c],
+            recv_sem=hop_recv.at[sender, c],
+            device_id=device(p, 3 - hub_z),
             device_id_type=MESH,
         )
 
-    own_right.wait()
-    for c in range(CHUNKS):
-        over_peers(lambda offset: right_copy(offset, c).wait_recv())
-
-        @pl.when(z < depth - 1)
-        def _():
-            hop(z, c, True, 0).start()
-
-        @pl.when(z > 0)
-        def _():
-            hop(z, c, False, 0).start()
+    @pl.when(is_hub)
+    def _():
+        own_left.start()
+        own_right.wait()
+        for c in range(CHUNKS):
+            over_peers(1, lambda offset: right_copy(offset, c, 0).wait_recv())
+            hop(hub_z, c, 0).start()
 
     lax.fori_loop(0, rows, gate_row, 0, unroll=UNROLL)
 
-    def pass_on(distance, c):
-        @pl.when(z >= distance)
-        def _():
-            hop(z - distance, c, True, distance - 1).wait_recv()
-
-        @pl.when((z >= distance) & (z < depth - 1))
-        def _():
-            hop(z - distance, c, True, distance).start()
-
-        @pl.when(z + distance < depth)
-        def _():
-            hop(z + distance, c, False, distance - 1).wait_recv()
-
-        @pl.when((z + distance < depth) & (z > 0))
-        def _():
-            hop(z + distance, c, False, distance).start()
-
-    near = z // (depth // 2)
-
-    def back_copy(r_to, side, c):
+    def back_copy(member, r_to, side, c):
         q = r_to * 2 + side
         offset = (q - p + plane) % plane
         return pltpu.make_async_remote_copy(
             src_ref=products.at[
-                side, pl.ds(c * step, step), pl.ds(pl.multiple_of(r_to * rows, rows), rows), :
+                member,
+                side,
+                pl.ds(c * step, step),
+                pl.ds(pl.multiple_of(r_to * rows, rows), rows),
+                :,
             ],
             dst_ref=returned.at[pl.ds(p * mine + c * step, step)],
-            send_sem=back_send.at[offset, c],
+            send_sem=back_send.at[member, offset, c],
             recv_sem=back_recv.at[offset, c],
-            device_id=device(q),
+            device_id=device(q, end_z if member else hub_z),
             device_id_type=MESH,
         )
 
-    def multiply(side, c):
+    def multiply(member, side, c):
         part = pl.ds(c * step, step)
         result = lax.dot_general(
-            lefts[part],
+            lefts[member, part],
             rights[part, pl.ds(pl.multiple_of(side * cols, cols), cols), :],
             (((2,), (2,)), ((0,), (0,))),
             preferred_element_type=jnp.float32,
         )
-        products[side, part] = result.astype(products.dtype)
+        products[member, side, part] = result.astype(products.dtype)
 
         def give(r_to, carry):
-            @pl.when(r_to * 2 + side != p)
-            def _():
-                back_copy(r_to, side, c).start()
+            if member:
+                back_copy(member, r_to, side, c).start()
+            else:
+
+                @pl.when(r_to * 2 + side != p)
+                def _():
+                    back_copy(member, r_to, side, c).start()
 
             return carry
 
         lax.fori_loop(0, PLANE_ROWS, give, 0)
 
+    own_back = pltpu.make_async_copy(
+        products.at[0, x, :, here_left, :], returned.at[pl.ds(p * mine, mine)], local_sem.at[2]
+    )
+
+    @pl.when(is_hub)
+    def _():
+        for c in range(CHUNKS):
+            over_peers(0, lambda offset: right_copy(offset, c, 1).wait_recv())
+            hop(end_z, c, 1).start()
+        own_left.wait()
+        over_peers(1, lambda offset: left_copy(offset, 0).wait_recv())
+        for c in range(CHUNKS):
+            multiply(0, pod, c)
+        over_peers(0, lambda offset: left_copy(offset, 1).wait_recv())
+        for c in range(CHUNKS):
+            multiply(1, pod, c)
+        for c in range(CHUNKS):
+            hop(3 - hub_z, c, 0).wait_recv()
+            hop(3 - end_z, c, 1).wait_recv()
+            multiply(1, 1 - pod, c)
+            multiply(0, 1 - pod, c)
+        own_back.start()
+        own_back.wait()
+
+    def back_of(member, offset, c):
+        q = peer(offset)
+        return back_copy(member, q // 2, q % 2, c)
+
     for c in range(CHUNKS):
-        pass_on(1, c)
-    own_left.wait()
-    over_peers(lambda offset: left_copy(offset).wait_recv())
-    for c in range(CHUNKS):
-        multiply(near, c)
-    for c in range(CHUNKS):
-        for distance in range(2, depth):
-            pass_on(distance, c)
-        multiply(1 - near, c)
-
-    own_back = pltpu.make_async_copy(
-        products.at[x, :, here_left, :], returned.at[pl.ds(p * mine, mine)], local_sem.at[2]
-    )
-    own_back.start()
-    own_back.wait()
-
-    def back_wait(offset, c, receive):
-        q = peer(offset)
-        copy = back_copy(q // 2, q % 2, c)
-        if receive:
-            copy.wait_recv()
-        else:
-            copy.wait_send()
-
-    for c in range(CHUNKS):
-        over_peers(lambda offset: back_wait(offset, c, True))
+        over_peers(first, lambda offset: back_of(0, offset, c).wait_recv())
     scaled[...] = centre(returned[...]).reshape(scaled.shape)
 
     def last_row(i, carry):
@@ -416,19 +412,16 @@
     out_ref[...] = staged[...].reshape(out_ref.shape).astype(out_ref.dtype)
 
     for c in range(CHUNKS):
-        over_peers(lambda offset: back_wait(offset, c, False))
-        over_peers(lambda offset: right_copy(offset, c).wait_send())
-        for distance in range(depth - 1):
-
-            @pl.when((z >= distance) & (z < depth - 1))
-            def _():
-                hop(z - distance, c, True, distance).wait_send()
-
-            @pl.when((z + distance < depth) & (z > 0))
-            def _():
-                hop(z + distance, c, False, distance).wait_send()
-
-    over_peers(lambda offset: left_copy(offset).wait_send())
+        over_peers(first, lambda offset: right_copy(offset, c, kind).wait_send())
+
+        @pl.when(is_hub)
+        def _():
+            over_peers(1, lambda offset: back_of(0, offset, c).wait_send())
+            over_peers(0, lambda offset: back_of(1, offset, c).wait_send())
+            hop(hub_z, c, 0).wait_send()
+            hop(end_z, c, 1).wait_send()
+
+    over_peers(first, lambda offset: left_copy(offset, kind).wait_send())
     swap.wait_send()
 
 
@@ -446,7 +439,7 @@
     columns = jnp.stack([norm_gain, norm_bias, out_gain, out_bias], axis=1)
     bf16, f32 = jnp.bfloat16, jnp.float32
     return pl.pallas_call(
-        functools.partial(triangle_kernel, depth),
+        triangle_kernel,
         out_shape=jax.ShapeDtypeStruct((channels, rows, cols), bf16),
         in_specs=[pl.BlockSpec(memory_space=pltpu.HBM)] * 6,
         out_specs=pl.BlockSpec(memory_space=pltpu.VMEM),
@@ -467,23 +460,21 @@
             pltpu.VMEM((rows, channels, cols), f32),
             pltpu.VMEM((hidden, rows, cols), bf16),
             pltpu.VMEM((hidden, rows, cols), bf16),
-            pltpu.VMEM((mine, tall, width), bf16),
+            pltpu.VMEM((2, mine, tall, width), bf16),
             pltpu.VMEM((mine, depth * tall, width), bf16),
-            pltpu.VMEM((2, mine, tall, cols), bf16),
+            pltpu.VMEM((2, 2, mine, tall, cols), bf16),
             pltpu.VMEM((hidden, rows, cols), bf16),
             dma((4,)),
             dma((5,)),
             dma(()),
             dma(()),
             dma((plane, CHUNKS)),
-            dma((plane, CHUNKS)),
+            dma((2, plane, CHUNKS)),
             dma((plane,)),
-            dma((plane,)),
-            dma((depth - 1, CHUNKS)),
-            dma((depth - 1, CHUNKS)),
-            dma((depth - 1, CHUNKS)),
-            dma((depth - 1, CHUNKS)),
-            dma((plane, CHUNKS)),
+            dma((2, plane)),
+            dma((2, CHUNKS)),
+            dma((2, CHUNKS)),
+            dma((2, plane, CHUNKS)),
             dma((plane, CHUNKS)),
         ],
         compiler_params=pltpu.CompilerParams(
@@ -497,7 +488,7 @@
     sizes = dict(mesh.shape)
     depth = sizes["res"] // PLANE_ROWS
     body = wide_body
-    if sizes["chan"] == 2 and sizes["res"] % PLANE_ROWS == 0 and depth in (2, 4):
+    if sizes["chan"] == 2 and sizes["res"] % PLANE_ROWS == 0 and depth == 4:
         body = functools.partial(plane_body, depth)
     return jax.shard_map(
         body,

time: 66.3 us -> 61 us (0.920); the launches traced: 65.1 us -> 60.9 us
  Pallas kernels: 60.9 us -> 57.5 us
  local copies, waits for them, and re-layouts: 4.18 us -> 3.3 us
    pallas_call x1, Pallas kernels: 60.9 us -> 57.5 us  [plane_body(): pl.pallas_call(triangle_kernel, out_shape=jax.ShapeDtypeStruct((channels,...]
    unnamed x19 -> x9, local copies, waits for them, and re-layouts: 4.07 us -> 2.56 us
where the time goes in v3:
time: 61 us; the launch traced here: 60.9 us
  Pallas kernels  57.5 us (94%)
  local copies, waits for them, and re-layouts  3.3 us (5%)
    pallas_call x1, Pallas kernels, plane_body(): pl.pallas_call(triangle_kernel, out_shape=jax.ShapeDtypeStruct((channels,...  57.5 us
    unnamed x9, local copies, waits for them, and re-layouts  2.56 us

profile of v3, /device:TPU:25, one launch (start us, length us, event | category | flops | bytes accessed | tf_op | source)
XLA Modules:
  0.0 60.9 jit_solution(13637699615347336224)
XLA Ops:
  0.0 0.0 copy-start.3
  0.0 0.0 copy-start
  0.0 0.0 copy-start.1
  0.0 0.0 copy-start.2
  0.0 0.6 %copy-done.3 = f32[128]{0:T(128)S(1)} copy-done((f32[128]{0:T(128)S(1)}, f32[128]{0:T(128)}, u32[]{:S(2)}) %copy-start.3) | copy-done | bytes 536
  0.7 0.0 copy-done
  0.7 0.0 copy-done.1
  0.7 0.0 copy-done.2
  0.7 0.7 %copy.14.columns_ref = f32[128,4]{1,0:T(8,128)} copy(f32[128,4]{0,1:T(4,128)S(1)} %pad_maximum_fusion) | data formatting | bytes 4096 | tf_op jit(solution)/shard_map/stack | solution.py:439
  1.5 57.5 %triangle.1 = bf16[128,16,128]{2,1,0:T(8,128)(2,1)} custom-call(bf16[64,16,256]{2,1,0:T(8,128)(2,1)} %pair_ref.1, s32[16,128]{1,0:T(8,128)} %mask_ref.1, f32[128,4]{1,0:T(8,128)} %copy.14.columns_ref, bf16[128,512]{1,0:T(8,128)(2,1)} %edges_ref.1, bf16[128,128]{1,0:T(8,128)(2,1)} %gate_ref.1, bf16[128,128]{1,0:T(8,128)(2,1)} %last_ref.1), custom_call_target="tpu_custom_call" | custom-call | tf_op jit(solution)/shard_map/triangle/pallas_call | solution.py:441
  59.0 1.9 %copy.16 = bf16[128,16,128]{2,1,0:T(8,128)(2,1)} copy(bf16[128,16,128]{2,1,0:T(8,128)(2,1)} %triangle.1) | data formatting | bytes 1048576
  (1 shorter events, 0.0 us)
Async XLA Ops:
  0.0 0.7 %copy-start.3 = (f32[128]{0:T(128)S(1)}, f32[128]{0:T(128)}, u32[]{:S(2)}) copy-start(f32[128]{0:T(128)} %param.11) | copy-start | bytes 1540
  0.0 0.7 %copy-start = (f32[128]{0:T(128)S(1)}, f32[128]{0:T(128)}, u32[]{:S(2)}) copy-start(f32[128]{0:T(128)} %param.16) | copy-start | bytes 1540
  0.0 0.7 %copy-start.1 = (f32[128]{0:T(128)S(1)}, f32[128]{0:T(128)}, u32[]{:S(2)}) copy-start(f32[128]{0:T(128)} %param.15) | copy-start | bytes 1540
  0.0 0.7 %copy-start.2 = (f32[128]{0:T(128)S(1)}, f32[128]{0:T(128)}, u32[]{:S(2)}) copy-start(f32[128]{0:T(128)} %param.12) | copy-start | bytes 1540

commit v4 on v3

--- a/solution.py
+++ b/solution.py
@@ -11,7 +11,7 @@
 MESH = pl.DeviceIdType.MESH
 PLANE_ROWS = 4
 CHUNKS = 4
-UNROLL = 2
+UNROLL = 16
 VMEM_LIMIT = 60 * 1024 * 1024
 
 
@@ -96,7 +96,10 @@
 def triangle_kernel(
     pair_ref,
     mask_ref,
-    columns_ref,
+    norm_gain_ref,
+    norm_bias_ref,
+    out_gain_ref,
+    out_bias_ref,
     edges_ref,
     gate_ref,
     last_ref,
@@ -149,7 +152,10 @@
         pltpu.make_async_copy(source, target, load_sem.at[index])
         for index, (source, target) in enumerate(
             (
-                (columns_ref, columns),
+                (norm_gain_ref, columns.at[0]),
+                (norm_bias_ref, columns.at[1]),
+                (out_gain_ref, columns.at[2]),
+                (out_bias_ref, columns.at[3]),
                 (edges_ref, edges),
                 (gate_ref, gate_weight),
                 (last_ref, last_weight),
@@ -216,7 +222,7 @@
     for load in loads:
         load.wait()
     for index in range(4):
-        wide[index] = jnp.broadcast_to(columns[:, index : index + 1], wide.shape[1:])
+        wide[index] = jnp.broadcast_to(columns[index], wide.shape[:0:-1]).T
     edges_t[...] = edges[...].T
     gate_t[...] = gate_weight[...].T
     last_t[...] = last_weight[...].T
@@ -436,17 +442,17 @@
     tall = PLANE_ROWS * rows
     dma = pltpu.SemaphoreType.DMA
 
-    columns = jnp.stack([norm_gain, norm_bias, out_gain, out_bias], axis=1)
+    columns = [v[None] for v in (norm_gain, norm_bias, out_gain, out_bias)]
     bf16, f32 = jnp.bfloat16, jnp.float32
     return pl.pallas_call(
         triangle_kernel,
         out_shape=jax.ShapeDtypeStruct((channels, rows, cols), bf16),
-        in_specs=[pl.BlockSpec(memory_space=pltpu.HBM)] * 6,
+        in_specs=[pl.BlockSpec(memory_space=pltpu.HBM)] * 9,
         out_specs=pl.BlockSpec(memory_space=pltpu.VMEM),
         scratch_shapes=[
             pltpu.VMEM((channels, rows, cols), bf16),
             pltpu.VMEM(pair_mask.shape, pair_mask.dtype),
-            pltpu.VMEM(columns.shape, f32),
+            pltpu.VMEM((4, 1, channels), f32),
             pltpu.VMEM(w_edges.shape, bf16),
             pltpu.VMEM(w_gate.shape, bf16),
             pltpu.VMEM(w_out.shape, bf16),
@@ -465,7 +471,7 @@
             pltpu.VMEM((2, 2, mine, tall, cols), bf16),
             pltpu.VMEM((hidden, rows, cols), bf16),
             dma((4,)),
-            dma((5,)),
+            dma((8,)),
             dma(()),
             dma(()),
             dma((plane, CHUNKS)),
@@ -481,7 +487,7 @@
             collective_id=1, has_side_effects=True, vmem_limit_bytes=VMEM_LIMIT
         ),
         name="triangle",
-    )(pair, pair_mask, columns, w_edges, w_gate, w_out)
+    )(pair, pair_mask, *columns, w_edges, w_gate, w_out)
 
 
 def solution(mesh):

time: 61 us -> 57.6 us (0.944)
  Pallas kernels: 57.5 us -> 55.5 us
  local copies, waits for them, and re-layouts: 3.3 us -> 1.87 us
    pallas_call x1, Pallas kernels: 57.5 us -> 55.5 us  [plane_body(): pl.pallas_call(triangle_kernel, out_shape=jax.ShapeDtypeStruct((channels,...]
    another operation x1 -> x0, local copies, waits for them, and re-layouts: 0.74 us -> none  [plane_body(): columns = jnp.stack([norm_gain, norm_bias, out_gain, out_bias], axis=1)]
    unnamed x9 -> x1, local copies, waits for them, and re-layouts: 2.56 us -> 1.87 us
where the time goes in v4:
time: 57.6 us; the launch traced here: 57.4 us
  Pallas kernels  55.5 us (96%)
  local copies, waits for them, and re-layouts  1.87 us (3%)
    pallas_call x1, Pallas kernels, plane_body(): pl.pallas_call(triangle_kernel, out_shape=jax.ShapeDtypeStruct((channels,...  55.5 us
    unnamed x1, local copies, waits for them, and re-layouts  1.87 us

profile of v4, /device:TPU:25, one launch (start us, length us, event | category | flops | bytes accessed | tf_op | source)
XLA Modules:
  0.0 57.4 jit_solution(991447027072285553)
XLA Ops:
  0.0 55.5 %triangle.1 = bf16[128,16,128]{2,1,0:T(8,128)(2,1)} custom-call(bf16[64,16,256]{2,1,0:T(8,128)(2,1)} %pair_ref.1, s32[16,128]{1,0:T(8,128)} %mask_ref.1, f32[1,128]{1,0:T(1,128)} %bitcast.4, f32[1,128]{1,0:T(1,128)} %bitcast.5, f32[1,128]{1,0:T(1,128)} %bitcast.6, f32[1,128]{1,0:T(1,128)} %bitcast.7, bf16[128,512]{1,0:T(8,128)(2,1)} %edges_ref.1, ...), custom_call_target="tpu_custom_call" | custom-call | tf_op jit(solution)/shard_map/triangle/pallas_call | solution.py:447
  55.6 1.9 %copy.11 = bf16[128,16,128]{2,1,0:T(8,128)(2,1)} copy(bf16[128,16,128]{2,1,0:T(8,128)(2,1)} %triangle.1) | data formatting | bytes 1048576

commit v5 on v4

--- a/solution.py
+++ b/solution.py
@@ -12,7 +12,7 @@
 PLANE_ROWS = 4
 CHUNKS = 4
 UNROLL = 16
-VMEM_LIMIT = 60 * 1024 * 1024
+VMEM_LIMIT = 52 * 1024 * 1024
 
 
 def layer_norm(values, scale_gain, shift_bias):
@@ -443,6 +443,10 @@
     dma = pltpu.SemaphoreType.DMA
 
     columns = [v[None] for v in (norm_gain, norm_bias, out_gain, out_bias)]
+    operands = [
+        pltpu.with_memory_space_constraint(operand, pltpu.HBM)
+        for operand in (pair, pair_mask, *columns, w_edges, w_gate, w_out)
+    ]
     bf16, f32 = jnp.bfloat16, jnp.float32
     return pl.pallas_call(
         triangle_kernel,
@@ -487,7 +491,7 @@
             collective_id=1, has_side_effects=True, vmem_limit_bytes=VMEM_LIMIT
         ),
         name="triangle",
-    )(pair, pair_mask, *columns, w_edges, w_gate, w_out)
+    )(*operands)
 
 
 def solution(mesh):

time: 57.6 us -> 55.7 us (0.967)
  local copies, waits for them, and re-layouts: 1.87 us -> 0.8 us
  Pallas kernels: 55.5 us -> 54.7 us
    unnamed x1, local copies, waits for them, and re-layouts: 1.87 us -> 0.8 us
    pallas_call x1, Pallas kernels: 55.5 us -> 54.7 us  [plane_body(): pl.pallas_call(triangle_kernel, out_shape=jax.ShapeDtypeStruct((channels,...]
where the time goes in v5:
time: 55.7 us; the launch traced here: 55.5 us
  Pallas kernels  54.7 us (98%)
  local copies, waits for them, and re-layouts  0.8 us (1%)
    pallas_call x1, Pallas kernels, plane_body(): pl.pallas_call(triangle_kernel, out_shape=jax.ShapeDtypeStruct((channels,...  54.7 us

profile of v5, /device:TPU:25, one launch (start us, length us, event | category | flops | bytes accessed | tf_op | source)
XLA Modules:
  0.0 55.5 jit_solution(9642003043213066491)
XLA Ops:
  0.0 54.7 %triangle.1 = bf16[128,16,128]{2,1,0:T(8,128)(2,1)S(1)} custom-call(bf16[64,16,256]{2,1,0:T(8,128)(2,1)} %pair_ref.1, s32[16,128]{1,0:T(8,128)} %mask_ref.1, f32[1,128]{1,0:T(1,128)} %bitcast.4, f32[1,128]{1,0:T(1,128)} %bitcast.5, f32[1,128]{1,0:T(1,128)} %bitcast.6, f32[1,128]{1,0:T(1,128)} %bitcast.7, bf16[128,512]{1,0:T(8,128)(2,1)} %edges_ref.1, ...), custom_call_target="tpu_custom_call" | custom-call | tf_op jit(solution)/shard_map/triangle/pallas_call | solution.py:451
  54.7 0.8 %copy.11 = bf16[128,16,128]{2,1,0:T(8,128)(2,1)} copy(bf16[128,16,128]{2,1,0:T(8,128)(2,1)S(1)} %triangle.1) | data formatting | bytes 1048576
